TPU v7x, 32 devices: a whole 2x2x4 slice. The times are simulated.
32 devices in a mesh: mode: 4 (over y, core), mesh: 8 (over z, x).
Axes of the slice: x: 2, y: 2, z: 4, core: 2. Of those that a mesh axis runs over, the one named last changes fastest.
Arguments:
- src_rows: bfloat16 [8192, 640], P(('mode', 'mesh')), parts along dimension 0, may hold values from -4 to 4
- src_owner: int32 [8192, 1], P(('mode', 'mesh')), parts along dimension 0, may hold values from 0 to 7; in each aligned block of 256 rows (0 to 255, 256 to 511, ...) at most 64 rows name the same one
- src_slot: int32 [8192], P(('mode', 'mesh')), parts along dimension 0, may hold values from 0 to 63
- neighbour_offset: int32 [2048, 6], P(('mode', 'mesh')), parts along dimension 0, may hold values from -16 to 16
- liner_face: int32 [2048], P(('mode', 'mesh')), parts along dimension 0, may hold values from 0 to 127
- admittance: float32 [8, 128], P('mode', 'mesh'), parts along dimension 0, may hold values from 0.2 to 1.5
- observe_weight: float32 [2048], P(('mode', 'mesh')), parts along dimension 0, may hold values from 0.3 to 3
- coupling: bfloat16 [24, 320, 640], P('mode'), parts along dimension 0, may hold values from -0.046875 to 0.046875
- block_inv: bfloat16 [1280, 640], P('mode'), parts along dimension 0, may hold values from -1.5 to 1.5, as said below
- liner_op: bfloat16 [1280, 640], P('mode'), parts along dimension 0, may hold values from -0.0625 to 0.0625
Outputs:
- state_field: bfloat16 [2048, 640], P(('mode', 'mesh')), parts along dimension 0
- adjoint_field: bfloat16 [2048, 640], P(('mode', 'mesh')), parts along dimension 0
- liner_grad: float32 [8, 128], P('mode', 'mesh'), parts along dimension 0
There are 4 independent parts, one for each index of `mode`. A program takes and returns all parts, laid end to end along the dimension named above; each array names one. Nothing has to cross between parts.
Inputs may be any that keep to these rules, and one draw needn't show every extreme that they name: `src_owner`: in the rows of one device no owner is named by more than 64 rows, a bound that some block reaches. `block_inv`: real parts of the diagonal entries lie near 0.8; the rest is of order 320 ** -0.5.
All inputs are finite; a program needn't handle non-finite values.
Results may differ from a plain program's by a relative error of at most 0.018.
Values may be sent and summed in bfloat16 or wider, within the bound.
A program may use at most 64 MiB of HBM per device.

v0:
```python
import functools

import jax
import jax.numpy as jnp
from jax import lax
from jax.experimental import pallas as pl
from jax.experimental.pallas import tpu as pltpu
from jax.sharding import PartitionSpec as P

SWEEPS = 4
RIM = 16
FACES = 6
HALF = 384
FULL = 2 * HALF
MESH = pl.DeviceIdType.MESH
F32 = jnp.float32
BF16 = jnp.bfloat16


def iota(shape, dim):
    return lax.broadcasted_iota(jnp.int32, shape, dim)


def dot(a, b):
    return jnp.dot(a, b, preferred_element_type=F32)


def widen(x, nb):
    rows = x.shape[0]
    turned = pltpu.roll(x, HALF - nb, 1)
    wrap = 2 * (HALF - nb)
    real = jnp.where(iota((rows, HALF), 1) < nb, x[:, :HALF], 0.0)
    last = jnp.where(iota((rows, wrap), 1) < HALF - nb, turned[:, :wrap], 0.0)
    return jnp.concatenate([real, turned[:, HALF:], last], axis=1)


def narrow(x, nb):
    turned = pltpu.roll(x, FULL - (HALF - nb), 1)
    return jnp.where(iota((x.shape[0], 2 * nb), 1) < nb, x[:, : 2 * nb], turned[:, : 2 * nb])


def combine(prod):
    rows = prod.shape[0] // 2
    return (
        prod[:rows, :HALF] - prod[rows:, HALF:],
        prod[:rows, HALF:] + prod[rows:, :HALF],
    )


def halves(x):
    return jnp.concatenate([x[:, :HALF], x[:, HALF:]], axis=0)


def column(row):
    count = row.shape[1]
    same = iota((count, count), 0) == iota((count, count), 1)
    return jnp.sum(jnp.where(same, row, 0.0), axis=1, keepdims=True)


def kernel(
    n,
    owner_ref,
    slot_ref,
    off_ref,
    face_ref,
    adm_ref,
    weight_ref,
    src_ref,
    coupling_ref,
    inv_ref,
    liner_ref,
    state_ref,
    adjoint_ref,
    grad_ref,
    send,
    recv,
    adm_send,
    adm_recv,
    off_send,
    off_halo,
    grad_send,
    grad_recv,
    fields,
    w_fwd,
    w_adj,
    inv_pad,
    inv_herm,
    liner_pad,
    matrix,
    pick_fwd,
    pick_adj,
    src_sems,
    adm_sems,
    off_sems,
    grad_sems,
    halo_sems,
):
    me = lax.axis_index("mesh")
    elems = off_ref.shape[1]
    nb = inv_ref.shape[0]
    lin = adm_ref.shape[1]
    rows = src_ref.shape[0]

    def peer(k):
        return lax.rem(me + k, n)

    def to(src, dst, send_sem, recv_sem, p):
        return pltpu.make_async_remote_copy(
            src_ref=src,
            dst_ref=dst,
            send_sem=send_sem,
            recv_sem=recv_sem,
            device_id={"mesh": p},
            device_id_type=MESH,
        )

    def src_copy(p, owner):
        return to(send.at[p], recv.at[owner], src_sems.at[0, p], src_sems.at[1, owner], p)

    def adm_copy(p, owner):
        return to(adm_send, adm_recv.at[owner], adm_sems.at[0, p], adm_sems.at[1, owner], p)

    def grad_copy(p, owner):
        return to(
            grad_send.at[p], grad_recv.at[owner], grad_sems.at[0, p], grad_sems.at[1, owner], p
        )

    def off_copy(side, p):
        return to(off_send, off_halo.at[side], off_sems.at[0, side], off_sems.at[1, side], p)

    def halo_copy(step, side, p):
        own = pl.ds(elems - RIM if side == 0 else 0, RIM)
        there = pl.ds(elems if side == 0 else elems + RIM, RIM)
        return to(
            fields.at[step, own],
            fields.at[step, there],
            halo_sems.at[0, step, side],
            halo_sems.at[1, step, side],
            p,
        )

    up, down = jnp.minimum(me + 1, n - 1), jnp.maximum(me - 1, 0)
    has_up, has_down = me < n - 1, me > 0

    fields[...] = jnp.zeros_like(fields)
    off_halo[...] = jnp.zeros_like(off_halo)

    barrier = pltpu.get_barrier_semaphore()

    @pl.loop(1, n)
    def _(k):
        pl.semaphore_signal(barrier, inc=1, device_id={"mesh": peer(k)}, device_id_type=MESH)

    adm_send[...] = jnp.zeros_like(adm_send)
    adm_send[0:2, 0:lin] = adm_ref[...]
    off_send[...] = jnp.zeros_like(off_send)
    off_send[0:FACES, 0:elems] = off_ref[...].astype(F32)
    target = owner_ref[...] * elems + slot_ref[...]

    def partial_sum(p):
        pick = (iota((elems, rows), 0) + p * elems) == target
        return dot(pick.astype(F32).astype(BF16), src_ref[...])

    pl.semaphore_wait(barrier, n - 1)

    @pl.loop(1, n)
    def _(k):
        p = peer(k)
        send[p] = partial_sum(p).astype(BF16)
        src_copy(p, me).start()

    @pl.when(has_up)
    def _():
        off_copy(0, up).start()

    @pl.when(has_down)
    def _():
        off_copy(1, down).start()

    @pl.loop(1, n)
    def _(k):
        adm_copy(peer(k), me).start()

    def padded(x):
        wide = widen(x.astype(F32), nb)
        return jnp.concatenate([wide, jnp.zeros((HALF - nb, FULL), F32)], axis=0)

    inv_wide = padded(inv_ref[...])
    inv_pad[...] = inv_wide.astype(BF16)
    inv_herm[:, :HALF] = inv_wide[:, :HALF].T.astype(BF16)
    inv_herm[:, HALF:] = (-inv_wide[:, HALF:].T).astype(BF16)
    liner_pad[...] = padded(liner_ref[...]).astype(BF16)

    def fold(f):
        at = pl.ds(pl.multiple_of(f * HALF, HALF), HALF)
        re, im = combine(dot(halves(matrix[...]), inv_pad[...]))
        w_fwd[at, :HALF] = re.astype(BF16)
        w_fwd[at, HALF:] = im.astype(BF16)
        re, im = combine(dot(halves(inv_pad[...]), matrix[...]))
        w_adj[at, :HALF] = re.T.astype(BF16)
        w_adj[at, HALF:] = (-im.T).astype(BF16)

    @pl.loop(0, FACES)
    def _(f):
        matrix[...] = padded(coupling_ref[f]).astype(BF16)
        fold(f)

    matrix[...] = liner_pad[...]
    fold(FACES)

    lane = iota((128, 128), 1)
    place_row = jnp.where(
        lane < elems,
        lane,
        jnp.where(
            lane < elems + RIM,
            lane - elems - RIM,
            jnp.where(lane < elems + 2 * RIM, lane - RIM, -4096),
        ),
    ).astype(F32)
    place_col = place_row.T
    for f in range(FACES):
        meets = lane[:1].astype(F32) + off_send[f : f + 1, :]
        pick_fwd[f * elems : (f + 1) * elems, :] = (
            jnp.where(place_col == meets, 1.0, 0.0).T[:elems].astype(BF16)
        )

    @pl.when(has_down)
    def _():
        off_copy(0, down).wait_recv()

    @pl.when(has_up)
    def _():
        off_copy(1, up).wait_recv()

    lane8 = iota((8, 128), 1)
    offs = jnp.where(
        lane8 < elems,
        off_send[...],
        jnp.where(
            lane8 < elems + RIM,
            pltpu.roll(off_halo[0], RIM, 1),
            pltpu.roll(off_halo[1], elems + RIM, 1),
        ),
    )
    for f in range(FACES):
        lands = place_row[:1] + offs[f : f + 1, :]
        pick_adj[f * elems : (f + 1) * elems, :] = jnp.where(
            iota((elems, 128), 0).astype(F32) == lands, 1.0, 0.0
        ).astype(BF16)

    face = column(face_ref[...].astype(F32))
    weight = column(weight_ref[...])
    lane_e = iota((elems, 128), 1)

    def face_pick(p):
        return jnp.logical_and(face == (lane_e + p * lin).astype(F32), lane_e < lin)

    def admit(table, p, sums):
        pick = face_pick(p)
        return tuple(s + jnp.where(pick, table[i : i + 1, :], 0.0) for i, s in enumerate(sums))

    def admit_peer(k, sums):
        p = peer(n - k)
        adm_copy(p, p).wait_recv()
        return admit(adm_recv[p], p, sums)

    sums = admit(adm_send[...], me, (jnp.zeros((elems, 128), F32),) * 2)
    sums = lax.fori_loop(1, n, admit_peer, sums)
    y_re = jnp.sum(sums[0], axis=1, keepdims=True)
    y_im = jnp.sum(sums[1], axis=1, keepdims=True)

    def take(k, total):
        p = peer(n - k)
        src_copy(p, p).wait_recv()
        return total + recv[p].astype(F32)

    forcing = widen(lax.fori_loop(1, n, take, partial_sum(me)), nb)

    def sweeps(first, start, pick_ref, w_ref, yi):
        start_re, start_im = start
        now_re, now_im = start
        for s in range(first, first + SWEEPS):
            now = jnp.concatenate([now_re, now_im], axis=1).astype(BF16)
            fields[s, 0:elems, :] = now

            @pl.when(has_up)
            def _():
                halo_copy(s, 0, up).start()

            @pl.when(has_down)
            def _():
                halo_copy(s, 1, down).start()

            u = now.astype(F32)
            u_re, u_im = u[:, :HALF], u[:, HALF:]
            wall = jnp.concatenate(
                [y_re * u_re - yi * u_im, y_re * u_im + yi * u_re], axis=0
            ).astype(BF16)

            @pl.when(has_down)
            def _():
                halo_copy(s, 0, down).wait_recv()

            @pl.when(has_up)
            def _():
                halo_copy(s, 1, up).wait_recv()

            met = dot(pick_ref[...], fields[s]).astype(BF16)
            parts = [halves(met[f * elems : (f + 1) * elems]) for f in range(FACES)]
            left = jnp.concatenate(parts + [wall], axis=1)
            re, im = combine(dot(left, w_ref[...]))
            now_re, now_im = start_re - re, start_im - im
        return jnp.concatenate([now_re, now_im], axis=1).astype(BF16)

    start = combine(dot(halves(forcing.astype(BF16)), inv_pad[...]))
    state = sweeps(0, start, pick_fwd, w_fwd, y_im)
    state_f = state.astype(F32)
    state_ref[...] = narrow(state_f, nb).astype(BF16)
    source = weight * state_f
    start = combine(dot(halves(source.astype(BF16)), inv_herm[...]))
    adjoint = sweeps(SWEEPS, start, pick_adj, w_adj, -y_im)
    adjoint_f = adjoint.astype(F32)
    adjoint_ref[...] = narrow(adjoint_f, nb).astype(BF16)

    wall_re, wall_im = combine(dot(halves(state), liner_pad[...]))
    a, b = adjoint_f[:, :HALF], adjoint_f[:, HALF:]
    term_re = -jnp.sum(a * wall_re + b * wall_im, axis=1, keepdims=True) / 16.0
    term_im = -jnp.sum(b * wall_re - a * wall_im, axis=1, keepdims=True) / 16.0

    def grad_part(p):
        pick = face_pick(p)
        re = jnp.sum(jnp.where(pick, term_re, 0.0), axis=0, keepdims=True)
        im = jnp.sum(jnp.where(pick, term_im, 0.0), axis=0, keepdims=True)
        return jnp.concatenate([re, im, jnp.zeros((6, 128), F32)], axis=0)

    @pl.loop(1, n)
    def _(k):
        p = peer(k)
        grad_send[p] = grad_part(p)
        grad_copy(p, me).start()

    def take_grad(k, total):
        p = peer(n - k)
        grad_copy(p, p).wait_recv()
        return total + grad_recv[p]

    total = lax.fori_loop(1, n, take_grad, grad_part(me))
    grad_ref[...] = total[0:2, 0:lin]

    @pl.loop(1, n)
    def _(k):
        p = peer(k)
        src_copy(p, me).wait_send()
        adm_copy(p, me).wait_send()
        grad_copy(p, me).wait_send()

    @pl.when(has_up)
    def _():
        off_copy(0, up).wait_send()
        for s in range(2 * SWEEPS):
            halo_copy(s, 0, up).wait_send()

    @pl.when(has_down)
    def _():
        off_copy(1, down).wait_send()
        for s in range(2 * SWEEPS):
            halo_copy(s, 1, down).wait_send()


def solution(mesh):
    n = mesh.shape["mesh"]

    def local(
        src_rows,
        src_owner,
        src_slot,
        neighbour_offset,
        liner_face,
        admittance,
        observe_weight,
        coupling,
        block_inv,
        liner_op,
    ):
        rows, width = src_rows.shape
        elems = liner_face.shape[0]
        lin = admittance.shape[1]
        vmem = pl.BlockSpec(memory_space=pltpu.VMEM)
        dma = pltpu.SemaphoreType.DMA
        return tuple(
            pl.pallas_call(
                functools.partial(kernel, n),
                out_shape=(
                    jax.ShapeDtypeStruct((elems, width), BF16),
                    jax.ShapeDtypeStruct((elems, width), BF16),
                    jax.ShapeDtypeStruct((2, lin), F32),
                ),
                in_specs=[vmem] * 10,
                out_specs=(vmem,) * 3,
                scratch_shapes=[
                    pltpu.VMEM((n, elems, width), BF16),
                    pltpu.VMEM((n, elems, width), BF16),
                    pltpu.VMEM((8, 128), F32),
                    pltpu.VMEM((n, 8, 128), F32),
                    pltpu.VMEM((8, 128), F32),
                    pltpu.VMEM((2, 8, 128), F32),
                    pltpu.VMEM((n, 8, 128), F32),
                    pltpu.VMEM((n, 8, 128), F32),
                    pltpu.VMEM((2 * SWEEPS, 128, FULL), BF16),
                    pltpu.VMEM(((FACES + 1) * HALF, FULL), BF16),
                    pltpu.VMEM(((FACES + 1) * HALF, FULL), BF16),
                    pltpu.VMEM((HALF, FULL), BF16),
                    pltpu.VMEM((HALF, FULL), BF16),
                    pltpu.VMEM((HALF, FULL), BF16),
                    pltpu.VMEM((HALF, FULL), BF16),
                    pltpu.VMEM((FACES * elems, 128), BF16),
                    pltpu.VMEM((FACES * elems, 128), BF16),
                    dma((2, n)),
                    dma((2, n)),
                    dma((2, 2)),
                    dma((2, n)),
                    dma((2, 2 * SWEEPS, 2)),
                ],
                compiler_params=pltpu.CompilerParams(
                    collective_id=0, has_side_effects=True, vmem_limit_bytes=48 * 2**20
                ),
            )(
                src_owner.reshape(1, rows),
                src_slot.reshape(1, rows),
                neighbour_offset.T,
                liner_face.reshape(1, elems),
                admittance,
                observe_weight.reshape(1, elems),
                src_rows,
                coupling,
                block_inv,
                liner_op,
            )
        )

    placed = (
        P(("mode", "mesh"), None),
        P(("mode", "mesh"), None),
        P(("mode", "mesh")),
        P(("mode", "mesh"), None),
        P(("mode", "mesh")),
        P("mode", "mesh"),
        P(("mode", "mesh")),
        P("mode", None, None),
        P("mode", None),
        P("mode", None),
    )
    return jax.shard_map(
        local,
        mesh=mesh,
        in_specs=placed,
        out_specs=(P(("mode", "mesh"), None), P(("mode", "mesh"), None), P("mode", "mesh")),
        check_vma=False,
    )
```

profile of v0, /device:TPU:0, one launch (start us, length us, event | category | flops | bytes accessed | tf_op | source)
XLA Modules:
  0.0 75.5 jit_solution(265576461903431522)
XLA Ops:
  0.6 0.0 copy-start
  0.6 1.7 %copy-done = bf16[6,320,640]{2,1,0:T(8,128)(2,1)S(1)} copy-done((bf16[6,320,640]{2,1,0:T(8,128)(2,1)S(1)}, bf16[6,320,640]{2,1,0:T(8,128)(2,1)}, u32[]{:S(2)}) %copy-start) | copy-done | bytes 2457624
  2.3 0.0 copy-start.1
  2.3 1.0 %copy-done.1 = bf16[320,640]{1,0:T(8,128)(2,1)S(1)} copy-done((bf16[320,640]{1,0:T(8,128)(2,1)S(1)}, bf16[320,640]{1,0:T(8,128)(2,1)}, u32[]{:S(2)}) %copy-start.1) | copy-done | bytes 409624
  3.3 0.0 copy-start.2
  3.3 1.0 %copy-done.2 = bf16[320,640]{1,0:T(8,128)(2,1)S(1)} copy-done((bf16[320,640]{1,0:T(8,128)(2,1)S(1)}, bf16[320,640]{1,0:T(8,128)(2,1)}, u32[]{:S(2)}) %copy-start.2) | copy-done | bytes 409624
  4.3 0.0 copy-start.3
  4.3 1.0 %copy-done.3 = bf16[256,640]{1,0:T(8,128)(2,1)S(1)} copy-done((bf16[256,640]{1,0:T(8,128)(2,1)S(1)}, bf16[256,640]{1,0:T(8,128)(2,1)}, u32[]{:S(2)}) %copy-start.3) | copy-done | bytes 327704
  5.3 0.0 copy-start.4
  5.3 0.7 copy-done.4
  6.0 0.0 copy-start.5
  6.0 0.7 copy-done.5
  6.7 0.0 copy-start.6
  6.7 0.7 copy-done.6
  7.4 0.0 copy-start.7
  7.4 0.7 copy-done.7
  8.0 0.0 copy-start.8
  8.0 0.7 copy-done.8
  8.7 0.0 copy-start.9
  8.7 0.7 copy-done.9
  9.3 64.3 %shard_map.121 = (bf16[64,640]{1,0:T(8,128)(2,1)S(1)}, bf16[64,640]{1,0:T(8,128)(2,1)S(1)}, f32[2,16]{1,0:T(2,128)S(1)}) custom-call(s32[1,256]{1,0:T(1,128)S(1)} %bitcast.6, s32[1,256]{1,0:T(1,128)S(1)} %bitcast.7, s32[6,64]{1,0:T(8,128)S(1)} %bitcast.5, s32[1,64]{1,0:T(1,128)S(1)} %bitcast.8, f32[2,16]{1,0:T(2,128)S(1)} %copy-done.7, f32[1,64]{1,0:T(1,128)S(1)} %bitcast.9, ...), custom_call_target="tpu_custom_call" | custom-call | tf_op jit(solution)/shard_map/pallas_call | solution.py:392
  73.7 0.6 copy.16
  74.3 0.6 copy.17
  75.0 0.6 copy.18
Async XLA Ops:
  0.6 1.7 %copy-start = (bf16[6,320,640]{2,1,0:T(8,128)(2,1)S(1)}, bf16[6,320,640]{2,1,0:T(8,128)(2,1)}, u32[]{:S(2)}) copy-start(bf16[6,320,640]{2,1,0:T(8,128)(2,1)} %coupling_ref.1) | copy-start | bytes 7372804
  2.3 1.0 %copy-start.1 = (bf16[320,640]{1,0:T(8,128)(2,1)S(1)}, bf16[320,640]{1,0:T(8,128)(2,1)}, u32[]{:S(2)}) copy-start(bf16[320,640]{1,0:T(8,128)(2,1)} %inv_ref.1) | copy-start | bytes 1228804
  3.3 1.0 %copy-start.2 = (bf16[320,640]{1,0:T(8,128)(2,1)S(1)}, bf16[320,640]{1,0:T(8,128)(2,1)}, u32[]{:S(2)}) copy-start(bf16[320,640]{1,0:T(8,128)(2,1)} %liner_ref.1) | copy-start | bytes 1228804
  4.3 1.0 %copy-start.3 = (bf16[256,640]{1,0:T(8,128)(2,1)S(1)}, bf16[256,640]{1,0:T(8,128)(2,1)}, u32[]{:S(2)}) copy-start(bf16[256,640]{1,0:T(8,128)(2,1)} %src_ref.1) | copy-start | bytes 983044
  5.3 0.7 copy-start.4
  6.0 0.7 copy-start.5
  6.7 0.7 copy-start.6
  7.4 0.7 copy-start.7
  8.0 0.7 copy-start.8
  8.7 0.7 copy-start.9
where the time goes:
time: 75.9 us; the launch traced here: 75.5 us
  Pallas kernels  64.3 us (85%)
  local copies, waits for them, and re-layouts  10.5 us (14%)
    pallas_call x1, Pallas kernels, local(): pl.pallas_call(functools.partial(kernel, n), out_shape=(jax.ShapeDtypeStr...  64.3 us
    unnamed x23, local copies, waits for them, and re-layouts  10.5 us

commit v1 on v0

--- a/solution.py
+++ b/solution.py
@@ -9,6 +9,7 @@
 
 SWEEPS = 4
 RIM = 16
+DEEP = 2 * RIM
 FACES = 6
 HALF = 384
 FULL = 2 * HALF
@@ -66,9 +67,9 @@
     adm_ref,
     weight_ref,
     src_ref,
-    coupling_ref,
-    inv_ref,
-    liner_ref,
+    coupling_hbm,
+    inv_hbm,
+    liner_hbm,
     state_ref,
     adjoint_ref,
     grad_ref,
@@ -94,12 +95,25 @@
     off_sems,
     grad_sems,
     halo_sems,
+    coupling_ref,
+    inv_ref,
+    liner_ref,
+    load_sems,
 ):
     me = lax.axis_index("mesh")
     elems = off_ref.shape[1]
     nb = inv_ref.shape[0]
     lin = adm_ref.shape[1]
     rows = src_ref.shape[0]
+
+    loads = [
+        pltpu.make_async_copy(hbm, here, load_sems.at[i])
+        for i, (hbm, here) in enumerate(
+            ((inv_hbm, inv_ref), (liner_hbm, liner_ref), (coupling_hbm, coupling_ref))
+        )
+    ]
+    for load in loads:
+        load.start()
 
     def peer(k):
         return lax.rem(me + k, n)
@@ -129,13 +143,13 @@
         return to(off_send, off_halo.at[side], off_sems.at[0, side], off_sems.at[1, side], p)
 
     def halo_copy(step, side, p):
-        own = pl.ds(elems - RIM if side == 0 else 0, RIM)
-        there = pl.ds(elems if side == 0 else elems + RIM, RIM)
+        own = pl.ds(elems - DEEP if side == 0 else 0, DEEP)
+        there = pl.ds(elems if side == 0 else elems + DEEP, DEEP)
         return to(
             fields.at[step, own],
             fields.at[step, there],
-            halo_sems.at[0, step, side],
-            halo_sems.at[1, step, side],
+            halo_sems.at[0, step // 2, side],
+            halo_sems.at[1, step // 2, side],
             p,
         )
 
@@ -155,6 +169,7 @@
     adm_send[0:2, 0:lin] = adm_ref[...]
     off_send[...] = jnp.zeros_like(off_send)
     off_send[0:FACES, 0:elems] = off_ref[...].astype(F32)
+    off_send[FACES : FACES + 1, 0:elems] = face_ref[...].astype(F32)
     target = owner_ref[...] * elems + slot_ref[...]
 
     def partial_sum(p):
@@ -185,6 +200,8 @@
         wide = widen(x.astype(F32), nb)
         return jnp.concatenate([wide, jnp.zeros((HALF - nb, FULL), F32)], axis=0)
 
+    for load in loads:
+        load.wait()
     inv_wide = padded(inv_ref[...])
     inv_pad[...] = inv_wide.astype(BF16)
     inv_herm[:, :HALF] = inv_wide[:, :HALF].T.astype(BF16)
@@ -208,23 +225,6 @@
     matrix[...] = liner_pad[...]
     fold(FACES)
 
-    lane = iota((128, 128), 1)
-    place_row = jnp.where(
-        lane < elems,
-        lane,
-        jnp.where(
-            lane < elems + RIM,
-            lane - elems - RIM,
-            jnp.where(lane < elems + 2 * RIM, lane - RIM, -4096),
-        ),
-    ).astype(F32)
-    place_col = place_row.T
-    for f in range(FACES):
-        meets = lane[:1].astype(F32) + off_send[f : f + 1, :]
-        pick_fwd[f * elems : (f + 1) * elems, :] = (
-            jnp.where(place_col == meets, 1.0, 0.0).T[:elems].astype(BF16)
-        )
-
     @pl.when(has_down)
     def _():
         off_copy(0, down).wait_recv()
@@ -238,26 +238,38 @@
         lane8 < elems,
         off_send[...],
         jnp.where(
-            lane8 < elems + RIM,
-            pltpu.roll(off_halo[0], RIM, 1),
-            pltpu.roll(off_halo[1], elems + RIM, 1),
+            lane8 < elems + DEEP,
+            pltpu.roll(off_halo[0], DEEP, 1),
+            pltpu.roll(off_halo[1], elems + DEEP, 1),
         ),
     )
+    lane = iota((128, 128), 1)
+    place_row = jnp.where(
+        lane < elems, lane, jnp.where(lane < elems + DEEP, lane - elems - DEEP, lane - DEEP)
+    ).astype(F32)
+    place_col = place_row.T
+    near = elems + DEEP - RIM
+
+    def kept(x):
+        return jnp.concatenate([x[:elems], x[near : near + DEEP]], axis=0)
+
     for f in range(FACES):
-        lands = place_row[:1] + offs[f : f + 1, :]
-        pick_adj[f * elems : (f + 1) * elems, :] = jnp.where(
-            iota((elems, 128), 0).astype(F32) == lands, 1.0, 0.0
-        ).astype(BF16)
-
-    face = column(face_ref[...].astype(F32))
+        lands = jnp.where(place_col == place_row + offs[f : f + 1, :], 1.0, 0.0)
+        pick_adj[f] = kept(lands).astype(BF16)
+        pick_fwd[f] = kept(lands.T).astype(BF16)
+
+    face_all = kept(column(offs[FACES : FACES + 1, :]))
+    face = face_all[:elems]
     weight = column(weight_ref[...])
     lane_e = iota((elems, 128), 1)
 
+    lane_a = iota((elems + DEEP, 128), 1)
+
     def face_pick(p):
         return jnp.logical_and(face == (lane_e + p * lin).astype(F32), lane_e < lin)
 
     def admit(table, p, sums):
-        pick = face_pick(p)
+        pick = jnp.logical_and(face_all == (lane_a + p * lin).astype(F32), lane_a < lin)
         return tuple(s + jnp.where(pick, table[i : i + 1, :], 0.0) for i, s in enumerate(sums))
 
     def admit_peer(k, sums):
@@ -265,7 +277,7 @@
         adm_copy(p, p).wait_recv()
         return admit(adm_recv[p], p, sums)
 
-    sums = admit(adm_send[...], me, (jnp.zeros((elems, 128), F32),) * 2)
+    sums = admit(adm_send[...], me, (jnp.zeros((elems + DEEP, 128), F32),) * 2)
     sums = lax.fori_loop(1, n, admit_peer, sums)
     y_re = jnp.sum(sums[0], axis=1, keepdims=True)
     y_im = jnp.sum(sums[1], axis=1, keepdims=True)
@@ -277,11 +289,20 @@
 
     forcing = widen(lax.fori_loop(1, n, take, partial_sum(me)), nb)
 
-    def sweeps(first, start, pick_ref, w_ref, yi):
-        start_re, start_im = start
-        now_re, now_im = start
-        for s in range(first, first + SWEEPS):
-            now = jnp.concatenate([now_re, now_im], axis=1).astype(BF16)
+    def sweeps(first, start, pick_ref, w_ref, yi, beside):
+        def sweep(s, pick, u, y_r, y_i):
+            count = u.shape[0]
+            u_re, u_im = u[:, :HALF], u[:, HALF:]
+            wall = jnp.concatenate([y_r * u_re - y_i * u_im, y_r * u_im + y_i * u_re], axis=0)
+            met = dot(pick.reshape(FACES * count, 128), fields[s]).astype(BF16)
+            parts = [halves(met[f * count : (f + 1) * count]) for f in range(FACES)]
+            left = jnp.concatenate(parts + [wall.astype(BF16)], axis=1)
+            return jnp.concatenate(combine(dot(left, w_ref[...])), axis=1)
+
+        start = jnp.concatenate(start, axis=1)
+        now = start.astype(BF16)
+        start_near = None
+        for s in range(first, first + SWEEPS, 2):
             fields[s, 0:elems, :] = now
 
             @pl.when(has_up)
@@ -292,11 +313,8 @@
             def _():
                 halo_copy(s, 1, down).start()
 
-            u = now.astype(F32)
-            u_re, u_im = u[:, :HALF], u[:, HALF:]
-            wall = jnp.concatenate(
-                [y_re * u_re - yi * u_im, y_re * u_im + yi * u_re], axis=0
-            ).astype(BF16)
+            if s == first:
+                beside()
 
             @pl.when(has_down)
             def _():
@@ -306,24 +324,32 @@
             def _():
                 halo_copy(s, 1, up).wait_recv()
 
-            met = dot(pick_ref[...], fields[s]).astype(BF16)
-            parts = [halves(met[f * elems : (f + 1) * elems]) for f in range(FACES)]
-            left = jnp.concatenate(parts + [wall], axis=1)
-            re, im = combine(dot(left, w_ref[...]))
-            now_re, now_im = start_re - re, start_im - im
-        return jnp.concatenate([now_re, now_im], axis=1).astype(BF16)
+            halo = fields[s, near : near + DEEP, :].astype(F32)
+            if start_near is None:
+                start_near = jnp.concatenate([start, halo], axis=0)
+            u = jnp.concatenate([now.astype(F32), halo], axis=0)
+            now = (start_near - sweep(s, pick_ref[...], u, y_re, yi)).astype(BF16)
+            fields[s + 1, 0:elems, :] = now[:elems]
+            fields[s + 1, near : near + DEEP, :] = now[elems:]
+            u = now[:elems].astype(F32)
+            now = start - sweep(s + 1, pick_ref[:, 0:elems, :], u, y_re[:elems], yi[:elems])
+            now = now.astype(BF16)
+        return now
 
     start = combine(dot(halves(forcing.astype(BF16)), inv_pad[...]))
-    state = sweeps(0, start, pick_fwd, w_fwd, y_im)
+    state = sweeps(0, start, pick_fwd, w_fwd, y_im, lambda: None)
     state_f = state.astype(F32)
-    state_ref[...] = narrow(state_f, nb).astype(BF16)
     source = weight * state_f
     start = combine(dot(halves(source.astype(BF16)), inv_herm[...]))
-    adjoint = sweeps(SWEEPS, start, pick_adj, w_adj, -y_im)
+    walls = []
+
+    def beside():
+        state_ref[...] = narrow(state_f, nb).astype(BF16)
+        walls.extend(combine(dot(halves(state), liner_pad[...])))
+
+    adjoint = sweeps(SWEEPS, start, pick_adj, w_adj, -y_im, beside)
     adjoint_f = adjoint.astype(F32)
-    adjoint_ref[...] = narrow(adjoint_f, nb).astype(BF16)
-
-    wall_re, wall_im = combine(dot(halves(state), liner_pad[...]))
+    wall_re, wall_im = walls
     a, b = adjoint_f[:, :HALF], adjoint_f[:, HALF:]
     term_re = -jnp.sum(a * wall_re + b * wall_im, axis=1, keepdims=True) / 16.0
     term_im = -jnp.sum(b * wall_re - a * wall_im, axis=1, keepdims=True) / 16.0
@@ -345,6 +371,7 @@
         grad_copy(p, p).wait_recv()
         return total + grad_recv[p]
 
+    adjoint_ref[...] = narrow(adjoint_f, nb).astype(BF16)
     total = lax.fori_loop(1, n, take_grad, grad_part(me))
     grad_ref[...] = total[0:2, 0:lin]
 
@@ -358,13 +385,13 @@
     @pl.when(has_up)
     def _():
         off_copy(0, up).wait_send()
-        for s in range(2 * SWEEPS):
+        for s in range(0, 2 * SWEEPS, 2):
             halo_copy(s, 0, up).wait_send()
 
     @pl.when(has_down)
     def _():
         off_copy(1, down).wait_send()
-        for s in range(2 * SWEEPS):
+        for s in range(0, 2 * SWEEPS, 2):
             halo_copy(s, 1, down).wait_send()
 
 
@@ -396,7 +423,7 @@
                     jax.ShapeDtypeStruct((elems, width), BF16),
                     jax.ShapeDtypeStruct((2, lin), F32),
                 ),
-                in_specs=[vmem] * 10,
+                in_specs=[vmem] * 7 + [pl.BlockSpec(memory_space=pltpu.HBM)] * 3,
                 out_specs=(vmem,) * 3,
                 scratch_shapes=[
                     pltpu.VMEM((n, elems, width), BF16),
@@ -414,16 +441,20 @@
                     pltpu.VMEM((HALF, FULL), BF16),
                     pltpu.VMEM((HALF, FULL), BF16),
                     pltpu.VMEM((HALF, FULL), BF16),
-                    pltpu.VMEM((FACES * elems, 128), BF16),
-                    pltpu.VMEM((FACES * elems, 128), BF16),
+                    pltpu.VMEM((FACES, elems + DEEP, 128), BF16),
+                    pltpu.VMEM((FACES, elems + DEEP, 128), BF16),
                     dma((2, n)),
                     dma((2, n)),
                     dma((2, 2)),
                     dma((2, n)),
-                    dma((2, 2 * SWEEPS, 2)),
+                    dma((2, SWEEPS, 2)),
+                    pltpu.VMEM(coupling.shape, BF16),
+                    pltpu.VMEM(block_inv.shape, BF16),
+                    pltpu.VMEM(liner_op.shape, BF16),
+                    dma((3,)),
                 ],
                 compiler_params=pltpu.CompilerParams(
-                    collective_id=0, has_side_effects=True, vmem_limit_bytes=48 * 2**20
+                    collective_id=0, has_side_effects=True, vmem_limit_bytes=2**26 - 2**16
                 ),
             )(
                 src_owner.reshape(1, rows),

time: 75.9 us -> 60.8 us (0.80)
  Pallas kernels: 64.3 us -> 55.7 us
  local copies, waits for them, and re-layouts: 10.5 us -> 4.26 us
    pallas_call x1, Pallas kernels: 64.3 us -> 55.7 us  [local(): pl.pallas_call(functools.partial(kernel, n), out_shape=(jax.ShapeDtypeStr...]
    unnamed x23 -> x3, local copies, waits for them, and re-layouts: 10.5 us -> 4.26 us
where the time goes in v1:
time: 60.8 us; the launch traced here: 60.6 us
  Pallas kernels  55.7 us (92%)
  local copies, waits for them, and re-layouts  4.26 us (7%)
  between operations  0.64 us (1%)
    pallas_call x1, Pallas kernels, local(): pl.pallas_call(functools.partial(kernel, n), out_shape=(jax.ShapeDtypeStr...  55.7 us
    unnamed x3, local copies, waits for them, and re-layouts  4.26 us

profile of v1, /device:TPU:0, one launch (start us, length us, event | category | flops | bytes accessed | tf_op | source)
XLA Modules:
  0.0 60.6 jit_solution(8504169462509827878)
XLA Ops:
  0.6 55.7 %shard_map.121 = (bf16[64,640]{1,0:T(8,128)(2,1)}, bf16[64,640]{1,0:T(8,128)(2,1)}, f32[2,16]{1,0:T(2,128)}) custom-call(s32[1,256]{1,0:T(1,128)} %bitcast.6, s32[1,256]{1,0:T(1,128)} %bitcast.7, s32[6,64]{1,0:T(8,128)} %bitcast.5, s32[1,64]{1,0:T(1,128)} %bitcast.8, f32[2,16]{1,0:T(2,128)} %adm_ref.1, f32[1,64]{1,0:T(1,128)} %bitcast.9, ...), custom_call_target="tpu_custom_call" | custom-call | tf_op jit(solution)/shard_map/pallas_call | solution.py:419
  56.3 1.5 %copy.16 = bf16[64,640]{1,0:T(8,128)(2,1)} copy(bf16[64,640]{1,0:T(8,128)(2,1)} %get-tuple-element.6) | data formatting | bytes 163840
  57.9 1.5 %copy.17 = bf16[64,640]{1,0:T(8,128)(2,1)} copy(bf16[64,640]{1,0:T(8,128)(2,1)} %get-tuple-element.7) | data formatting | bytes 163840
  59.4 1.2 %copy.18 = f32[2,16]{1,0:T(2,128)} copy(f32[2,16]{1,0:T(2,128)} %get-tuple-element.8) | data formatting | bytes 256

commit v2 on v1

--- a/solution.py
+++ b/solution.py
@@ -176,13 +176,16 @@
         pick = (iota((elems, rows), 0) + p * elems) == target
         return dot(pick.astype(F32).astype(BF16), src_ref[...])
 
-    pl.semaphore_wait(barrier, n - 1)
-
     @pl.loop(1, n)
     def _(k):
         p = peer(k)
         send[p] = partial_sum(p).astype(BF16)
-        src_copy(p, me).start()
+
+    pl.semaphore_wait(barrier, n - 1)
+
+    @pl.loop(1, n)
+    def _(k):
+        src_copy(peer(k), me).start()
 
     @pl.when(has_up)
     def _():

time: 60.8 us -> 60.5 us (level)
  no operation moved by 1% of the time
where the time goes in v2:
time: 60.5 us; the launch traced here: 60.2 us
  Pallas kernels  55.3 us (91%)
  local copies, waits for them, and re-layouts  4.26 us (7%)
  between operations  0.64 us (1%)
    pallas_call x1, Pallas kernels, local(): pl.pallas_call(functools.partial(kernel, n), out_shape=(jax.ShapeDtypeStr...  55.3 us
    unnamed x3, local copies, waits for them, and re-layouts  4.26 us

profile of v2, /device:TPU:0, one launch (start us, length us, event | category | flops | bytes accessed | tf_op | source)
XLA Modules:
  0.0 60.2 jit_solution(1810163925018918124)
XLA Ops:
  0.6 55.3 %shard_map.121 = (bf16[64,640]{1,0:T(8,128)(2,1)}, bf16[64,640]{1,0:T(8,128)(2,1)}, f32[2,16]{1,0:T(2,128)}) custom-call(s32[1,256]{1,0:T(1,128)} %bitcast.6, s32[1,256]{1,0:T(1,128)} %bitcast.7, s32[6,64]{1,0:T(8,128)} %bitcast.5, s32[1,64]{1,0:T(1,128)} %bitcast.8, f32[2,16]{1,0:T(2,128)} %adm_ref.1, f32[1,64]{1,0:T(1,128)} %bitcast.9, ...), custom_call_target="tpu_custom_call" | custom-call | tf_op jit(solution)/shard_map/pallas_call | solution.py:422
  56.0 1.5 %copy.16 = bf16[64,640]{1,0:T(8,128)(2,1)} copy(bf16[64,640]{1,0:T(8,128)(2,1)} %get-tuple-element.6) | data formatting | bytes 163840
  57.5 1.5 %copy.17 = bf16[64,640]{1,0:T(8,128)(2,1)} copy(bf16[64,640]{1,0:T(8,128)(2,1)} %get-tuple-element.7) | data formatting | bytes 163840
  59.0 1.2 %copy.18 = f32[2,16]{1,0:T(2,128)} copy(f32[2,16]{1,0:T(2,128)} %get-tuple-element.8) | data formatting | bytes 256
